TPU v7x, 32 devices: a whole 2x2x4 slice. The times are simulated.
32 devices in a mesh: row: 8 (over z, y), col: 4 (over x, core).
Axes of the slice: x: 2, y: 2, z: 4, core: 2. Of those that a mesh axis runs over, the one named last changes fastest.
Arguments:
- activations: bfloat16 [8192, 4096], P(('row', 'col')), may hold values from -6 to 6
- out_grads: bfloat16 [8192, 4096], P(('row', 'col')), may hold values from -6 to 6
- proj_in: bfloat16 [4096, 128], replicated, may hold values from -0.09375 to 0.09375
- proj_out: bfloat16 [4096, 128], replicated, may hold values from -0.09375 to 0.09375
- lengths: int32 [256], P(('row', 'col')), may hold values from 1 to 32, 6144 in all
- gram_old: float32 [16384, 16384], P('row', 'col'), as said below
- queries: float32 [16384, 256], P('row'), may hold values from -96 to 96
Outputs:
- gram_new: float32 [16384, 16384], P('row', 'col')
- solution: float32 [16384, 256], P('row')
Inputs may be any that keep to these rules, and one draw needn't show every extreme that they name: `gram_old`: symmetric and positive definite. Example e's token slots from lengths[e] on are padding.
All inputs are finite; a program needn't handle non-finite values. No bound on the sum of `lengths` on one device may be relied on, other than what follows from the above.
Results may differ from a plain program's by a relative error of at most 0.0055.
Values may be sent and summed in bfloat16 or wider, within the bound.
No kernel may reach another device: no remote copies, remote signals or barrier semaphores. Data moves between devices by JAX's collectives and lax.ppermute only.
A program may use at most 192 MiB of HBM per device.

v0:
```python
import jax
import jax.numpy as jnp
from jax import lax
from jax.sharding import PartitionSpec as P

SEQ = 32
ITERS = 2


decay_rate = 0.5
damping = 1.0


def spread(value, axis, root):
    mine = lax.axis_index(axis) == root
    return lax.psum(jnp.where(mine, value, jnp.zeros_like(value)), axis)


def shards(activations, out_grads, proj_in, proj_out, lengths, gram_old, queries):
    local_count = lengths.shape[0]
    proj_rank = proj_in.shape[1]
    features = proj_rank * proj_rank
    row_count = lax.axis_size("row")
    col_count = lax.axis_size("col")
    row_block = gram_old.shape[0]
    col_block = gram_old.shape[1]
    row_start = lax.axis_index("row") * row_block
    col_start = lax.axis_index("col") * col_block
    low_in = jnp.dot(activations, proj_in, preferred_element_type=jnp.float32).astype(jnp.bfloat16)
    low_out = jnp.dot(out_grads, proj_out, preferred_element_type=jnp.float32).astype(jnp.bfloat16)
    low_in = low_in.reshape(local_count, SEQ, proj_rank)
    low_out = low_out.reshape(local_count, SEQ, proj_rank)
    valid_mask = jnp.arange(SEQ)[None, :] < lengths[:, None]
    low_out = jnp.where(valid_mask[:, :, None], low_out, jnp.zeros((), jnp.bfloat16))
    local_grads = jnp.einsum(
        "eto,eti->eoi", low_out.astype(jnp.float32), low_in.astype(jnp.float32)
    )
    local_grads = local_grads.reshape(local_count, features).astype(jnp.bfloat16)
    shard_rows = lax.all_gather(local_grads, ("row", "col"), axis=0, tiled=True)
    left_part = lax.dynamic_slice_in_dim(shard_rows, row_start, row_block, 1)
    right_part = lax.dynamic_slice_in_dim(shard_rows, col_start, col_block, 1)
    product = lax.dot_general(
        left_part, right_part, (((0,), (0,)), ((), ())), preferred_element_type=jnp.float32
    )
    total_examples = local_count * row_count * col_count
    gram_new = decay_rate * gram_old + (1.0 - decay_rate) / total_examples * product
    rows_global = row_start + jnp.arange(row_block, dtype=jnp.int32)
    cols_global = col_start + jnp.arange(col_block, dtype=jnp.int32)
    gram_new = gram_new + jnp.where(
        rows_global[:, None] == cols_global[None, :], damping, 0.0
    ).astype(jnp.float32)

    def operate(vector_block):
        blocks_per_col = row_count // col_count
        members = []
        for member in range(blocks_per_col):
            members.append(
                spread(vector_block, "row", blocks_per_col * lax.axis_index("col") + member)
            )
        col_part = jnp.concatenate(members, 0)
        partial_value = jnp.dot(
            gram_new, col_part, precision=lax.Precision.HIGHEST, preferred_element_type=jnp.float32
        )
        return lax.psum(partial_value, "col")

    def paired_sums(residual, mapped):
        return lax.psum(
            (jnp.sum(residual * residual, axis=0), jnp.sum(residual * mapped, axis=0)), "row"
        )

    solution = jnp.zeros_like(queries)
    residual = queries
    mapped = operate(residual)
    norm_now, curvature_sum = paired_sums(residual, mapped)
    step_size = norm_now / curvature_sum
    direction = residual
    along = mapped
    for sweep in range(ITERS):
        solution = solution + step_size * direction
        if sweep + 1 < ITERS:
            residual = residual - step_size * along
            mapped = operate(residual)
            norm_next, curvature_sum = paired_sums(residual, mapped)
            momentum = norm_next / norm_now
            step_size = norm_next / (curvature_sum - momentum * norm_next / step_size)
            direction = residual + momentum * direction
            along = mapped + momentum * along
            norm_now = norm_next
    return (gram_new, solution)


def solution(mesh):
    in_specs = (
        P(("row", "col"), None),
        P(("row", "col"), None),
        P(),
        P(),
        P(("row", "col")),
        P("row", "col"),
        P("row", None),
    )
    out_specs = (P("row", "col"), P("row", None))
    return jax.shard_map(shards, mesh=mesh, in_specs=in_specs, out_specs=out_specs, check_vma=False)
```

profile of v0, /device:TPU:0, one launch (start us, length us, event | category | flops | bytes accessed | tf_op | source)
XLA Modules:
  0.0 576.8 jit_solution(5136280661189231055)
XLA Ops:
  8.0 0.0 all-gather.2.cloned.1.call-start
  8.1 0.9 iota_compare_fusion
  9.0 0.7 copy-done
  9.6 1.9 convolution_convert_fusion.2
  11.6 0.7 convolution_convert_fusion.1
  12.3 0.3 fusion.9
  12.6 0.9 copy.11
  13.5 0.0 all-reduce.15.cloned.1.call-start
  13.6 2.3 broadcast_select_fusion.3
  15.9 0.0 all-reduce.15.cloned.1.call-update
  15.9 0.0 all-reduce.9.cloned.1.call-start
  16.0 116.9 %all-gather.2.cloned.1.call-done = bf16[256,16384]{1,0:T(8,128)(2,1)} async-done(((bf16[8,16384]{1,0:T(8,128)(2,1)}), bf16[256,16384]{1,0:T(8,128)(2,1)}) %all-gather.2.cloned.1.call-update) | async-done | bytes 8388624 | tf_op jit(solution)/shard_map/all_gather | solution.py:39
  132.9 24.2 %select_add_fusion = f32[2048,4096]{1,0:T(8,128)} fusion(f32[2048,4096]{1,0:T(8,128)} %param.12, s32[4096]{0:T(1024)S(1)} %iota_add_fusion, s32[2048]{0:T(1024)S(1)} %iota_add_fusion.1, bf16[256,16384]{1,0:T(8,128)(2,1)} %all-gather.2.cloned.1.call-done, s32[]{:T(128)S(6)} %select_n.38, s32[]{:T(128)S(6)} %select_n.37), kind=kOutput, calls=%fused_computation | convolution fusion | flops 4345298944 | bytes 70279176 | tf_op jit(solution)/shard_map/dot_general | solution.py:42
  157.1 39.0 %all-reduce.15.cloned.1.call-done = (f32[2048,256]{1,0:T(8,128)}, f32[2048,256]{1,0:T(8,128)}) async-done(((f32[2048,256]{1,0:T(8,128)}, f32[2048,256]{1,0:T(8,128)}), (f32[2048,256]{1,0:T(8,128)}, f32[2048,256]{1,0:T(8,128)})) %all-reduce.15.cloned.1.call-update) | async-done | bytes 4194320 | tf_op jit(solution)/shard_map/psum | solution.py:16
  196.1 31.9 %fusion = f32[2048,256]{1,0:T(8,128)} fusion(f32[2048,4096]{1,0:T(8,128)} %select_add_fusion, f32[2048,256]{1,0:T(8,128)} %get-tuple-element.12, f32[2048,256]{1,0:T(8,128)} %get-tuple-element.13), kind=kOutput, calls=%fused_computation.1 | convolution fusion | flops 25770852352 | bytes 39845888 | tf_op jit(solution)/shard_map/dot_general | solution.py:61
  227.9 0.0 all-reduce.9.cloned.1.call-update
  228.0 0.0 all-reduce.13.cloned.1.call-start
  228.0 50.2 %all-reduce.9.cloned.1.call-done = f32[2048,256]{1,0:T(8,128)} async-done(((f32[2048,256]{1,0:T(8,128)}), f32[2048,256]{1,0:T(8,128)}) %all-reduce.9.cloned.1.call-update) | async-done | bytes 2097168 | tf_op jit(solution)/shard_map/psum | solution.py:64
  278.2 1.9 multiply_reduce_fusion.2
  280.1 21.4 %all-reduce.1 = (f32[256]{0:T(256)S(1)}, f32[256]{0:T(256)S(1)}) all-reduce(f32[256]{0:T(256)S(1)} %get-tuple-element.5, f32[256]{0:T(256)S(1)} %get-tuple-element.4), channel_id=1, replica_groups=mesh['row'=8,'col'=4] {'row'}, use_global_device_ids=true, to_apply=%region_1.2 | all-reduce | flops 512 | bytes 4096 | tf_op jit(solution)/shard_map/psum | solution.py:67
  301.5 3.3 broadcast_select_fusion.1
  304.8 1.6 broadcast_select_fusion
  306.3 0.4 copy-done.3
  306.7 0.0 all-reduce.13.cloned.1.call-update
  306.8 0.2 all-reduce.11.cloned.1.call-start
  307.0 152.7 %all-reduce.13.cloned.1.call-done = (f32[2048,256]{1,0:T(8,128)}, f32[2048,256]{1,0:T(8,128)}) async-done(((f32[2048,256]{1,0:T(8,128)}, f32[2048,256]{1,0:T(8,128)}), (f32[2048,256]{1,0:T(8,128)}, f32[2048,256]{1,0:T(8,128)})) %all-reduce.13.cloned.1.call-update) | async-done | bytes 4194320 | tf_op jit(solution)/shard_map/psum | solution.py:16
  459.7 31.9 %fusion.4 = f32[2048,256]{1,0:T(8,128)} fusion(f32[2048,4096]{1,0:T(8,128)} %select_add_fusion, f32[2048,256]{1,0:T(8,128)} %get-tuple-element.10, f32[2048,256]{1,0:T(8,128)} %get-tuple-element.11), kind=kOutput, calls=%fused_computation.5 | convolution fusion | flops 25770852352 | bytes 39845888 | tf_op jit(solution)/shard_map/dot_general | solution.py:61
  491.6 0.0 all-reduce.11.cloned.1.call-update
  491.6 50.3 %all-reduce.11.cloned.1.call-done = f32[2048,256]{1,0:T(8,128)} async-done(((f32[2048,256]{1,0:T(8,128)}), f32[2048,256]{1,0:T(8,128)}) %all-reduce.11.cloned.1.call-update) | async-done | bytes 2097168 | tf_op jit(solution)/shard_map/psum | solution.py:64
  541.9 1.9 multiply_reduce_fusion
  543.8 21.4 %all-reduce = (f32[256]{0:T(256)S(1)}, f32[256]{0:T(256)S(1)}) all-reduce(f32[256]{0:T(256)S(1)} %get-tuple-element.3, f32[256]{0:T(256)S(1)} %get-tuple-element.2), channel_id=1, replica_groups=mesh['row'=8,'col'=4] {'row'}, use_global_device_ids=true, to_apply=%region_8.9 | all-reduce | flops 512 | bytes 4096 | tf_op jit(solution)/shard_map/psum | solution.py:67
  565.2 4.0 multiply_add_fusion
  (17 shorter events, 0.1 us)
Async XLA Ops:
  8.0 1.6 copy-start
  8.0 3.5 copy-start.6
  8.0 124.9 %all-gather.2.cloned.1.call-start = ((), (), s32[]{:S(2)}) async-start(), calls=%async_computation | async-start | bytes 8650752 | tf_op jit(solution)/shard_map/all_gather | solution.py:39
  8.1 3.5 copy-start.5
  11.6 2.0 copy-start.2
  13.5 182.5 %all-reduce.15.cloned.1.call-start = ((), (), s32[]{:S(2)}) async-start(), calls=%async_computation.4 | async-start | bytes 8388608 | tf_op jit(solution)/shard_map/psum | solution.py:16
  15.9 262.3 %all-reduce.9.cloned.1.call-start = ((), (), s32[]{:S(2)}) async-start(), calls=%async_computation.1 | async-start | bytes 4194304 | tf_op jit(solution)/shard_map/psum | solution.py:64
  228.0 231.8 %all-reduce.13.cloned.1.call-start = ((), (), s32[]{:S(2)}) async-start(), calls=%async_computation.3 | async-start | bytes 8388608 | tf_op jit(solution)/shard_map/psum | solution.py:16
  304.8 2.0 copy-start.3
  306.8 235.1 %all-reduce.11.cloned.1.call-start = ((), (), s32[]{:S(2)}) async-start(), calls=%async_computation.2 | async-start | bytes 4194304 | tf_op jit(solution)/shard_map/psum | solution.py:64
  491.6 50.3 %copy-start.4 = (f32[2048,256]{1,0:T(8,128)S(1)}, f32[2048,256]{1,0:T(8,128)}, u32[]{:S(2)}) copy-start(f32[2048,256]{1,0:T(8,128)} %copy-done.3) | copy-start | bytes 6291460
  565.2 4.0 copy-start.1
Sparse Core Ops, SparseCore 0:
  13.6 119.2 all-gather.1
Sparse Core Ops, SparseCore 1:
  18.3 177.7 all-reduce.14
  228.0 50.1 all-reduce.8
  306.9 152.8 all-reduce.12
  491.7 50.1 all-reduce.10
where the time goes:
time: 577 us
  waiting for transfers between devices  409 us (71%)
  matrix products  90.9 us (16%)
  blocking collectives  42.7 us (7%)
  other arithmetic  15.9 us (3%)
  between operations  15.8 us (3%)
    psum x2, waiting for transfers between devices, spread(): return lax.psum(jnp.where(mine, value, jnp.zeros_like(value)), axis)  192 us
    all_gather x1, waiting for transfers between devices, shards(): shard_rows = lax.all_gather(local_grads, ('row', 'col'), axis=0, tiled=True)  117 us
    psum x2, waiting for transfers between devices, operate(): return lax.psum(partial_value, 'col')  100 us
    dot_general x2, matrix products, operate(): jnp.dot(gram_new, col_part, precision=lax.Precision.HIGHEST, preferred_el...  63.7 us
    psum x2, blocking collectives, paired_sums(): lax.psum((jnp.sum(residual * residual, axis=0), jnp.sum(residual * mapped...  42.7 us
    dot_general x1, matrix products, shards(): lax.dot_general(left_part, right_part, (((0,), (0,)), ((), ())), preferre...  24.2 us
  transfers between devices with their start and end apart: 5, of which 5 were waited for; matrix products, arithmetic and copies ran while one was open for 5% of the time, Pallas kernels for 0%

commit v1 on v0

v1 whole, which is shorter than its diff:
```python
import functools

import jax
import jax.numpy as jnp
from jax import lax
from jax.experimental import pallas as pl
from jax.experimental.pallas import tpu as pltpu
from jax.sharding import PartitionSpec as P

SEQ = 32

decay_rate = 0.5
damping = 1.0

BF = jnp.bfloat16
F32 = jnp.float32
VMEM_BYTES = 40 * 1024 * 1024


def dot(a, b, dims=((1,), (0,))):
    return lax.dot_general(a, b, (dims, ((), ())), preferred_element_type=F32)


def grads_kernel(chunks, outs, sel_ref, low_in_ref, out_ref):
    tokens = low_in_ref.shape[1]
    rank = low_in_ref.shape[2]
    slots = tokens // SEQ
    halves = sel_ref.shape[1]
    width = sel_ref.shape[3]
    example = lax.broadcasted_iota(jnp.int32, (slots, width), 0)
    token = lax.broadcasted_iota(jnp.int32, (slots, width), 1)
    pieces = []
    for j in range(chunks):
        left = []
        for h in range(halves):
            mask = ((token + h * width) // SEQ == example).astype(F32)
            rows = sel_ref[j, h]
            spread = rows[:, None, :] * mask[None, :, :]
            left.append(spread.reshape(outs * slots, width).astype(BF))
        left = jnp.concatenate(left, axis=1)
        pieces.append(dot(left, low_in_ref[j]).reshape(outs, slots, rank))
    both = jnp.concatenate(pieces, axis=1).astype(BF)
    for o in range(outs):
        out_ref[:, o * rank : (o + 1) * rank] = both[o]


def build_grads(sel, low_in):
    count, halves, outs, width = sel.shape
    _, tokens, rank = low_in.shape
    chunks = 2
    slots = tokens // SEQ
    return pl.pallas_call(
        functools.partial(grads_kernel, chunks, outs),
        grid=(count // chunks,),
        in_specs=[
            pl.BlockSpec((chunks, halves, outs, width), lambda i: (i, 0, 0, 0)),
            pl.BlockSpec((chunks, tokens, rank), lambda i: (i, 0, 0)),
        ],
        out_specs=pl.BlockSpec((chunks * slots, outs * rank), lambda i: (i, 0)),
        out_shape=jax.ShapeDtypeStruct((count * slots, outs * rank), BF),
        compiler_params=pltpu.CompilerParams(vmem_limit_bytes=VMEM_BYTES),
        cost_estimate=pl.CostEstimate(
            flops=2 * count * outs * slots * tokens * rank,
            bytes_accessed=count * (slots * outs * rank * 2 + tokens * rank * 4),
            transcendentals=0,
        ),
        name="build_grads",
    )(sel, low_in)


def old_product_kernel(first, half_ref, gram_ref, vec_ref, *rest):
    out_ref = rest[-1]
    block = gram_ref[...]
    high = block.astype(BF)
    low = (block - high.astype(F32)).astype(BF)
    vec = vec_ref[...]
    total = dot(high, vec) + dot(low, vec)
    if first:
        out_ref[...] = decay_rate * total
    else:
        out_ref[...] = rest[0][...] + decay_rate * total


def old_product(half, gram, vec, before=None):
    rows, cols = gram.shape
    depth, queries = vec.shape
    block = min(256, rows)
    in_specs = [
        pl.BlockSpec((block, depth), lambda i, half_ref: (i, half_ref[0])),
        pl.BlockSpec((depth, queries), lambda i, half_ref: (0, 0)),
    ]
    args = [gram, vec]
    if before is not None:
        in_specs.append(pl.BlockSpec((block, queries), lambda i, half_ref: (i, 0)))
        args.append(before)
    return pl.pallas_call(
        functools.partial(old_product_kernel, before is None),
        grid_spec=pltpu.PrefetchScalarGridSpec(
            num_scalar_prefetch=1,
            grid=(rows // block,),
            in_specs=in_specs,
            out_specs=pl.BlockSpec((block, queries), lambda i, half_ref: (i, 0)),
        ),
        out_shape=jax.ShapeDtypeStruct((rows, queries), F32),
        compiler_params=pltpu.CompilerParams(vmem_limit_bytes=VMEM_BYTES),
        cost_estimate=pl.CostEstimate(
            flops=4 * rows * depth * queries,
            bytes_accessed=4 * rows * depth + 2 * depth * queries + 4 * rows * queries,
            transcendentals=0,
        ),
        name="old_product",
    )(half, *args)


def gram_kernel(scale, block, strip, at_ref, gram_ref, left_ref, right_ref, out_ref):
    cols = gram_ref.shape[1]
    left = left_ref[...]
    offset = at_ref[0] + pl.program_id(0) * block
    ahead = lax.broadcasted_iota(jnp.int32, (block, strip), 0)
    ahead = ahead - lax.broadcasted_iota(jnp.int32, (block, strip), 1)
    for s in range(cols // strip):
        part = slice(s * strip, (s + 1) * strip)
        product = dot(left, right_ref[:, part], ((0,), (0,)))
        value = decay_rate * gram_ref[:, part] + scale * product
        out_ref[:, part] = value + jnp.where(ahead == s * strip - offset, damping, 0.0)


def update_gram(at, gram, grads, scale):
    rows, cols = gram.shape
    examples = grads.shape[0]
    block = min(256, rows)
    strip = min(1024, cols)
    return pl.pallas_call(
        functools.partial(gram_kernel, scale, block, strip),
        grid_spec=pltpu.PrefetchScalarGridSpec(
            num_scalar_prefetch=1,
            grid=(rows // block,),
            in_specs=[
                pl.BlockSpec((block, cols), lambda i, at_ref: (i, 0)),
                pl.BlockSpec((examples, block), lambda i, at_ref: (0, cols // block + i)),
                pl.BlockSpec((examples, cols), lambda i, at_ref: (0, 0)),
            ],
            out_specs=pl.BlockSpec((block, cols), lambda i, at_ref: (i, 0)),
        ),
        out_shape=jax.ShapeDtypeStruct((rows, cols), F32),
        compiler_params=pltpu.CompilerParams(vmem_limit_bytes=VMEM_BYTES),
        cost_estimate=pl.CostEstimate(
            flops=2 * rows * cols * examples,
            bytes_accessed=8 * rows * cols + 2 * examples * (rows + cols),
            transcendentals=0,
        ),
        name="update_gram",
    )(at, gram, grads, grads)


def moment_kernel(plan_ref, gram_ref, vec_ref, other_ref, left_ref, out_ref):
    part = pl.program_id(0)
    step = pl.program_id(1)

    @pl.when((part == 0) & (step == 0))
    def _():
        out_ref[...] = jnp.zeros_like(out_ref)

    def add(vec, weight):
        mapped = dot(gram_ref[...].astype(BF), vec) * left_ref[...]
        rows, queries = mapped.shape
        out_ref[...] += weight * jnp.sum(mapped.reshape(rows // 8, 8, queries), axis=0)

    @pl.when(part == 0)
    def _():
        add(vec_ref[...], plan_ref[2].astype(F32))

    @pl.when((part == 1) & (plan_ref[1] == 1))
    def _():
        add(other_ref[...], 1.0)


def moment(plan, gram, vec, other, left):
    rows, cols = gram.shape
    depth, queries = vec.shape
    block = min(256, rows)
    last = rows // block - 1

    def gram_at(p, i, plan_ref):
        skip = (p == 1) & (plan_ref[1] == 0)
        half = jnp.where((p == 1) & (plan_ref[1] == 1), 1 - plan_ref[0], plan_ref[0])
        return (jnp.where(skip, last, i), half)

    def left_at(p, i, plan_ref):
        return (jnp.where((p == 1) & (plan_ref[1] == 0), last, i), 0)

    return pl.pallas_call(
        moment_kernel,
        grid_spec=pltpu.PrefetchScalarGridSpec(
            num_scalar_prefetch=1,
            grid=(2, rows // block),
            in_specs=[
                pl.BlockSpec((block, depth), gram_at),
                pl.BlockSpec((depth, queries), lambda p, i, plan_ref: (0, 0)),
                pl.BlockSpec((depth, queries), lambda p, i, plan_ref: (0, 0)),
                pl.BlockSpec((block, queries), left_at),
            ],
            out_specs=pl.BlockSpec((8, queries), lambda p, i, plan_ref: (0, 0)),
        ),
        out_shape=jax.ShapeDtypeStruct((8, queries), F32),
        compiler_params=pltpu.CompilerParams(vmem_limit_bytes=VMEM_BYTES),
        cost_estimate=pl.CostEstimate(
            flops=2 * rows * cols * queries,
            bytes_accessed=4 * rows * cols + 8 * rows * queries,
            transcendentals=0,
        ),
        name="moment",
    )(plan, gram, vec, other, left)


def turn(value, position, axis):
    count = value.shape[axis]
    slots = [
        lax.dynamic_index_in_dim(value, (position - i) % count, axis, keepdims=True)
        for i in range(count)
    ]
    return jnp.concatenate(slots, axis)


def shards(activations, out_grads, proj_in, proj_out, lengths, gram_old, queries):
    local_count = lengths.shape[0]
    rank = proj_in.shape[1]
    row_count = lax.axis_size("row")
    col_count = lax.axis_size("col")
    rows, cols = gram_old.shape
    tokens = local_count * SEQ
    half_tokens = tokens // 2
    tiers = row_count // 2
    files = col_count // 2
    row = lax.axis_index("row")
    col = lax.axis_index("col")
    z, y = row // 2, row % 2
    x, core = col // 2, col % 2
    total_examples = local_count * row_count * col_count
    scale = (1.0 - decay_rate) / total_examples

    def move(value, goes):
        pairs = []
        for r in range(row_count):
            for c in range(col_count):
                to = goes(r // 2, r % 2, c // 2, c % 2)
                if to is not None:
                    pairs.append((r * col_count + c, (to[0] * 2 + to[1]) * col_count + to[2] * 2 + to[3]))
        return lax.ppermute(value, ("row", "col"), pairs)

    def swap_y(value):
        return move(value, lambda z, y, x, k: (z, 1 - y, x, k))

    def swap_core(value):
        return move(value, lambda z, y, x, k: (z, y, x, 1 - k))

    def ring_z(value):
        return move(value, lambda z, y, x, k: ((z + 1) % tiers, y, x, k))

    def ring_x(value):
        return move(value, lambda z, y, x, k: (z, y, (x + 1) % files, k))

    def flip_x(value, bit):
        return move(value, lambda z, y, x, k: (z, y, x ^ bit, k))

    def flip_z(value, bit):
        return move(value, lambda z, y, x, k: (z ^ bit, y, x, k))

    def chain(value, sign):
        got = []
        for s in range(1, tiers):

            def goes(z, y, x, k, s=s):
                source = x * 2 + k
                if z == source + sign * (s - 1) and 0 <= z + sign < tiers:
                    return (z + sign, y, x, k)
                return None

            value = move(value, goes)
            got.append(value)
        return got

    def ring(value, step, count):
        got = [value]
        for _ in range(count - 1):
            value = step(value)
            got.append(value)
        return got

    away = z - col
    sent = queries.astype(BF)
    ups, downs = chain(sent, 1), chain(sent, -1)
    mine = sent
    for s in range(1, tiers):
        mine = jnp.where(away == s, ups[s - 1], mine)
        mine = jnp.where(away == -s, downs[s - 1], mine)
    theirs = swap_y(mine)

    low_in = dot(activations, proj_in).astype(BF)
    low_out = dot(proj_out, out_grads, ((0,), (1,))).astype(BF)
    slot = jnp.arange(tokens, dtype=jnp.int32)
    valid_mask = slot % SEQ < jnp.repeat(lengths, SEQ)
    low_out = jnp.where(valid_mask[None, :], low_out, jnp.zeros((), BF))
    low_out = low_out.reshape(rank, 2, half_tokens).transpose(1, 0, 2)

    ins = jnp.stack(ring(low_in, ring_z, tiers))
    outs = jnp.stack(ring(low_out, ring_z, tiers))
    ins = jnp.stack([ins, swap_y(ins)])
    outs = jnp.stack(ring(outs, ring_x, files))
    ins = jnp.stack(ring(ins, ring_x, files))
    outs = jnp.stack([outs, swap_y(outs)])
    outs = jnp.swapaxes(outs, 0, 1)
    ins = jnp.stack([ins, swap_core(ins)])
    outs = jnp.stack([outs, swap_core(outs)])
    chunks = 2 * files * 2 * tiers
    ins = ins.reshape(chunks, tokens, rank)
    outs = outs.reshape(chunks, 2, rank, half_tokens)
    outs_col = cols // rank
    outs_row = rows // rank
    sel = jnp.concatenate(
        [
            lax.dynamic_slice_in_dim(outs, col * outs_col, outs_col, 2),
            lax.dynamic_slice_in_dim(outs, row * outs_row, outs_row, 2),
        ],
        axis=2,
    ).astype(F32)
    grads = build_grads(sel, ins)

    half = y.reshape(1).astype(jnp.int32)
    partial_value = old_product(half, gram_old, mine)
    partial_value = old_product(1 - half, gram_old, theirs, partial_value)
    halved = rows // 2
    give = lax.dynamic_slice_in_dim(partial_value, (1 - core) * halved, halved, 0)
    keep = lax.dynamic_slice_in_dim(partial_value, core * halved, halved, 0)
    keep = keep + swap_core(give)
    bit = 1
    while bit < files:
        short = keep.astype(BF)
        keep = short.astype(F32) + flip_x(short, bit).astype(F32)
        bit *= 2
    other = swap_core(keep)
    mapped = jnp.where(
        core == 0, jnp.concatenate([keep, other], 0), jnp.concatenate([other, keep], 0)
    )

    first = jnp.where(y == 0, mine, theirs)
    second = jnp.where(y == 0, theirs, mine)
    depth = rows
    inner = dot(grads[:, :depth], first) + dot(grads[:, depth:cols], second)
    count = inner.shape[1]
    inner = inner.reshape(2, files, -1, count)
    inner = turn(turn(inner, core, 0), x, 1)
    inner = inner + swap_core(inner)
    bit = 1
    while bit < files:
        inner = inner + flip_x(inner, bit)
        bit *= 2
    inner = turn(turn(inner, core, 0), x, 1).reshape(-1, count).astype(BF)
    mapped = mapped + scale * dot(grads[:, cols:], inner, ((0,), (0,))) + damping * queries

    at = (row * rows - col * cols).reshape(1).astype(jnp.int32)
    gram_new = update_gram(at, gram_old, grads, scale)

    short = mapped.astype(BF)

    def cross_at_source(z, y, x, k):
        return (z, 1 - y, x, k) if z == x * 2 + k else None

    cross = move(short, cross_at_source)
    ups, downs = chain(cross, 1), chain(short, -1)
    vec = short
    for s in range(1, tiers):
        vec = jnp.where(away == s, ups[s - 1], vec)
        vec = jnp.where(away == -s, downs[s - 1], vec)
    plan = jnp.stack(
        [
            jnp.where(away > 0, 1 - y, y),
            jnp.where(away == 0, 1, 0),
            jnp.where(away == 0, 1, 2),
        ]
    ).astype(jnp.int32)
    curve = jnp.sum(moment(plan, gram_new, vec, cross, mapped), axis=0)

    even = 1.0 / col_count
    sums = jnp.stack(
        [
            jnp.sum(queries * queries, axis=0) * even,
            jnp.sum(queries * mapped, axis=0) * even,
            jnp.sum(mapped * mapped, axis=0) * even,
            curve,
        ]
    )
    sums = sums + swap_core(sums)
    bit = 1
    while bit < files:
        sums = sums + flip_x(sums, bit)
        bit *= 2
    sums = sums + swap_y(sums)
    bit = 1
    while bit < tiers:
        sums = sums + flip_z(sums, bit)
        bit *= 2
    norm_now, along, square, curve = sums[0], sums[1], sums[2], sums[3]
    step = norm_now / along
    norm_next = step * step * square - norm_now
    momentum = norm_next / norm_now
    curvature = along - 2.0 * step * square + step * step * curve
    step_next = norm_next / (curvature - momentum * norm_next / step)
    solution = (step + step_next * (1.0 + momentum)) * queries - (step_next * step) * mapped
    return (gram_new, solution)


def solution(mesh):
    in_specs = (
        P(("row", "col"), None),
        P(("row", "col"), None),
        P(),
        P(),
        P(("row", "col")),
        P("row", "col"),
        P("row", None),
    )
    out_specs = (P("row", "col"), P("row", None))
    return jax.shard_map(shards, mesh=mesh, in_specs=in_specs, out_specs=out_specs, check_vma=False)
```

time: 577 us -> 262 us (0.45)
  waiting for transfers between devices: 409 us -> 91.1 us
  matrix products: 90.9 us -> 9.25 us
  Pallas kernels: 0 us -> 70.9 us
  starting transfers between devices: 0.39 us -> 69 us
  blocking collectives: 42.7 us -> 0 us
  between operations: 15.8 us -> 1.24 us
    psum x4 -> x0, waiting for transfers between devices: 292 us -> none  [the longest x2 192 us: spread(): return lax.psum(jnp.where(mine, value, jnp.zeros_like(value)), axis)]
    all_gather x1 -> x0, waiting for transfers between devices: 117 us -> none  [shards(): shard_rows = lax.all_gather(local_grads, ('row', 'col'), axis=0, tiled=True)]
    ppermute x0 -> x36, waiting for transfers between devices: none -> 91.1 us  [move(): return lax.ppermute(value, ('row', 'col'), pairs)]
    dot_general x6 -> x5, matrix products: 90.9 us -> 9.25 us  [dot(): return lax.dot_general(a, b, (dims, ((), ())), preferred_element_type=F32)]
    pallas_call x0 -> x5, Pallas kernels: none -> 70.9 us  [the longest x1 26.1 us: update_gram(): pl.pallas_call(functools.partial(gram_kernel, scale, block, strip), grid_...]
    ppermute x0 -> x36, starting transfers between devices: none -> 69 us  [move(): return lax.ppermute(value, ('row', 'col'), pairs)]
    psum x2 -> x0, blocking collectives: 42.7 us -> none  [paired_sums(): lax.psum((jnp.sum(residual * residual, axis=0), jnp.sum(residual * mapped...]
    select_n x3 -> x2, other arithmetic: 7.15 us -> 0.77 us  [the longest x1 0.42 us: shards(): mine = jnp.where(away == -s, downs[s - 1], mine)]
  transfers between devices with their start and end apart: 5 -> 36, of which waited for: 5 -> 17; matrix products, arithmetic and copies ran while one was open for 5% -> 5% of each run, Pallas kernels for 0% -> 20%
where the time goes in v1:
time: 262 us; the launch traced here: 261 us
  waiting for transfers between devices  91.1 us (35%)
  Pallas kernels  70.9 us (27%)
  starting transfers between devices  69 us (26%)
  other arithmetic  16 us (6%)
  matrix products  9.25 us (4%)
  local copies, waits for them, and re-layouts  3.6 us (1%)
    ppermute x36, waiting for transfers between devices, move(): return lax.ppermute(value, ('row', 'col'), pairs)  91.1 us
    ppermute x36, starting transfers between devices, move(): return lax.ppermute(value, ('row', 'col'), pairs)  69 us
    pallas_call x1, Pallas kernels, update_gram(): pl.pallas_call(functools.partial(gram_kernel, scale, block, strip), grid_...  26.1 us
    pallas_call x2, Pallas kernels, old_product(): pl.pallas_call(functools.partial(old_product_kernel, before is None), gri...  21.3 us
    pallas_call x1, Pallas kernels, moment(): pl.pallas_call(moment_kernel, grid_spec=pltpu.PrefetchScalarGridSpec(num_...  18.9 us
    dot_general x5, matrix products, dot(): return lax.dot_general(a, b, (dims, ((), ())), preferred_element_type=F32)  9.25 us
  transfers between devices with their start and end apart: 36, of which 17 were waited for; matrix products, arithmetic and copies ran while one was open for 5% of the time, Pallas kernels for 20%

profile of v1, /device:TPU:0, one launch (start us, length us, event | category | flops | bytes accessed | tf_op | source)
XLA Modules:
  0.0 261.2 jit_solution(17666056698321733181)
XLA Ops:
  0.7 1.8 convert_element_type.31
  2.5 6.0 %collective-permute-start.15 = (bf16[2048,256]{1,0:T(8,128)(2,1)S(1)}, bf16[2048,256]{1,0:T(8,128)(2,1)}, u32[]{:S(2)}, u32[]{:S(2)}) collective-permute-start(bf16[2048,256]{1,0:T(8,128)(2,1)S(1)} %convert_element_type.31), channel_id=1, source_target_pairs={{0,8},{4,12},{9,17},{13,21},{18,26},{22,30}} | collective-permute-start | bytes 3145736 | tf_op jit(solution)/shard_map/ppermute | solution.py:249
  8.6 1.7 collective-permute-start.12
  10.2 9.7 %collective-permute-done.15 = bf16[2048,256]{1,0:T(8,128)(2,1)} collective-permute-done((bf16[2048,256]{1,0:T(8,128)(2,1)S(1)}, bf16[2048,256]{1,0:T(8,128)(2,1)}, u32[]{:S(2)}, u32[]{:S(2)}) %collective-permute-start.15) | collective-permute-done | bytes 1048608 | tf_op jit(solution)/shard_map/ppermute | solution.py:249
  23.9 3.3 %collective-permute-start.6 = (bf16[256,128]{1,0:T(8,128)(2,1)S(1)}, bf16[256,128]{1,0:T(8,128)(2,1)S(1)}, u32[]{:S(2)}, u32[]{:S(2)}) collective-permute-start(bf16[256,128]{1,0:T(8,128)(2,1)S(1)} %convolution_convert_fusion), channel_id=1, source_target_pairs={{0,8},{1,9},{2,10},{3,11},{4,12},{5,13},{6,14},{7,15},{8,16},{9,17... | collective-permute-start | bytes 196616 | tf_op jit(solution)/shard_map/ppermute | solution.py:249
  30.6 2.4 fusion.3
  33.1 9.8 %collective-permute-start = (bf16[2,128,128]{2,1,0:T(8,128)(2,1)S(1)}, bf16[2,128,128]{2,1,0:T(8,128)(2,1)S(1)}, u32[]{:S(2)}, u32[]{:S(2)}) collective-permute-start(bf16[2,128,128]{2,1,0:T(8,128)(2,1)S(1)} %bitcast.68), channel_id=1, source_target_pairs={{0,8},{1,9},{2,10},{3,11},{4,12},{5,13},{6,14},{7,15},{8,16},{9,17... | collective-permute-start | bytes 196616 | tf_op jit(solution)/shard_map/ppermute | solution.py:249
  42.9 3.1 %collective-permute-start.7 = (bf16[256,128]{1,0:T(8,128)(2,1)S(1)}, bf16[256,128]{1,0:T(8,128)(2,1)S(1)}, u32[]{:S(2)}, u32[]{:S(2)}) collective-permute-start(bf16[256,128]{1,0:T(8,128)(2,1)S(1)} %collective-permute-done.6), channel_id=1, source_target_pairs={{0,8},{1,9},{2,10},{3,11},{4,12},{5,13},{6,14},{7,15},{8,16},{9,17... | collective-permute-start | bytes 196616 | tf_op jit(solution)/shard_map/ppermute | solution.py:249
  46.0 1.9 collective-permute-start.1
  49.3 8.3 %collective-permute-start.8 = (bf16[256,128]{1,0:T(8,128)(2,1)S(1)}, bf16[256,128]{1,0:T(8,128)(2,1)S(1)}, u32[]{:S(2)}, u32[]{:S(2)}) collective-permute-start(bf16[256,128]{1,0:T(8,128)(2,1)S(1)} %collective-permute-done.7), channel_id=1, source_target_pairs={{0,8},{1,9},{2,10},{3,11},{4,12},{5,13},{6,14},{7,15},{8,16},{9,17... | collective-permute-start | bytes 196616 | tf_op jit(solution)/shard_map/ppermute | solution.py:249
  57.6 3.6 %collective-permute-done.1 = bf16[2,128,128]{2,1,0:T(8,128)(2,1)S(1)} collective-permute-done((bf16[2,128,128]{2,1,0:T(8,128)(2,1)S(1)}, bf16[2,128,128]{2,1,0:T(8,128)(2,1)S(1)}, u32[]{:S(2)}, u32[]{:S(2)}) %collective-permute-start.1) | collective-permute-done | bytes 65568 | tf_op jit(solution)/shard_map/ppermute | solution.py:249
  63.5 3.7 %collective-permute-done.2 = bf16[2,128,128]{2,1,0:T(8,128)(2,1)S(1)} collective-permute-done((bf16[2,128,128]{2,1,0:T(8,128)(2,1)S(1)}, bf16[2,128,128]{2,1,0:T(8,128)(2,1)S(1)}, u32[]{:S(2)}, u32[]{:S(2)}) %collective-permute-start.2) | collective-permute-done | bytes 65568 | tf_op jit(solution)/shard_map/ppermute | solution.py:249
  67.4 2.4 collective-permute-done.9
  70.9 3.0 %collective-permute-done.3 = bf16[4,2,128,128]{3,2,1,0:T(8,128)(2,1)} collective-permute-done((bf16[4,2,128,128]{3,2,1,0:T(8,128)(2,1)S(1)}, bf16[4,2,128,128]{3,2,1,0:T(8,128)(2,1)}, u32[]{:S(2)}, u32[]{:S(2)}) %collective-permute-start.3) | collective-permute-done | bytes 262176 | tf_op jit(solution)/shard_map/ppermute | solution.py:249
  73.8 2.0 fusion.29
  78.4 12.6 %collective-permute-done.4 = bf16[2,4,2,128,128]{4,3,2,1,0:T(8,128)(2,1)} collective-permute-done((bf16[2,4,2,128,128]{4,3,2,1,0:T(8,128)(2,1)}, bf16[2,4,2,128,128]{4,3,2,1,0:T(8,128)(2,1)}, u32[]{:S(2)}, u32[]{:S(2)}) %collective-permute-start.4) | collective-permute-done | bytes 524320 | tf_op jit(solution)/shard_map/ppermute | solution.py:249
  94.1 10.5 %old_product.2.rest_0_ = f32[2048,256]{1,0:T(8,128)S(1)} custom-call(s32[1]{0:T(128)} %bitcast.27.half_ref, f32[2048,4096]{1,0:T(8,128)} %gram_ref.5, bf16[2048,256]{1,0:T(8,128)(2,1)S(1)} %select_select_fusion.1.vec_ref), custom_call_target="tpu_custom_call" | custom-call | flops 4294967296 | bytes 19922944 | tf_op jit(solution)/shard_map/old_product/pallas_call | solution.py:96
  104.6 10.9 %old_product.3 = f32[2048,256]{1,0:T(8,128)S(1)} custom-call(s32[1]{0:T(128)S(6)} %sub.49.half_ref, f32[2048,4096]{1,0:T(8,128)} %gram_ref.5, bf16[2048,256]{1,0:T(8,128)(2,1)S(1)} %collective-permute-done.18.vec_ref, f32[2048,256]{1,0:T(8,128)S(1)} %old_product.2.rest_0_), custom_call_target="tpu_custom_call" | custom-call | flops 4294967296 | bytes 19922944 | tf_op jit(solution)/shard_map/old_product/pallas_call | solution.py:96
  116.4 4.6 %build_grads.1.left_ref.right_ref = bf16[256,6144]{1,0:T(8,128)(2,1)S(1)} custom-call(f32[32,2,48,128]{3,2,1,0:T(8,128)S(1)} %maximum_convert_fusion.sel_ref, bf16[32,256,128]{2,1,0:T(8,128)(2,1)S(1)} %bitcast.62), custom_call_target="tpu_custom_call" | custom-call | flops 805306368 | bytes 7340032 | tf_op jit(solution)/shard_map/build_grads/pallas_call | solution.py:52
  122.8 13.2 %collective-permute-done.20 = bf16[1024,256]{1,0:T(8,128)(2,1)S(1)} collective-permute-done((bf16[1024,256]{1,0:T(8,128)(2,1)S(1)}, bf16[1024,256]{1,0:T(8,128)(2,1)S(1)}, u32[]{:S(2)}, u32[]{:S(2)}) %collective-permute-start.20) | collective-permute-done | bytes 524320 | tf_op jit(solution)/shard_map/ppermute | solution.py:249
  138.8 8.7 %collective-permute-done.23 = f32[2,2,64,256]{3,2,1,0:T(8,128)} collective-permute-done((f32[2,2,64,256]{3,2,1,0:T(8,128)}, f32[2,2,64,256]{3,2,1,0:T(8,128)}, u32[]{:S(2)}, u32[]{:S(2)}) %collective-permute-start.23) | collective-permute-done | bytes 262176 | tf_op jit(solution)/shard_map/ppermute | solution.py:249
  148.7 5.2 %multiply_reduce_fusion.2 = (f32[256]{0:T(256)S(1)}, f32[256]{0:T(256)S(1)}, f32[256]{0:T(256)S(1)}, bf16[2048,256]{1,0:T(8,128)(2,1)S(1)}, f32[2048,256]{1,0:T(8,128)}) fusion(f32[2048,256]{1,0:T(8,128)} %param.13, bf16[256,256]{1,0:T(8,128)(2,1)S(1)} %bitcast.72, bf16[256,6144]{1,0:T(8,128)(2,1)S(1)} %build_grads.1.left_ref.right_ref, ...), kind=kOutput, calls=%fused_computation.9 | convolution fusion | flops 275250432 | bytes 8522753 | tf_op jit(solution)/shard_map/dot_general | solution.py:21
  153.9 3.4 %collective-permute-start.27 = (bf16[2048,256]{1,0:T(8,128)(2,1)S(1)}, bf16[2048,256]{1,0:T(8,128)(2,1)S(1)}, u32[]{:S(2)}, u32[]{:S(2)}) collective-permute-start(bf16[2048,256]{1,0:T(8,128)(2,1)S(1)} %get-tuple-element.9), channel_id=1, source_target_pairs={{0,4},{4,0},{9,13},{13,9},{18,22},{22,18},{27,31},{31,27}} | collective-permute-start | bytes 3145736 | tf_op jit(solution)/shard_map/ppermute | solution.py:249
  158.0 12.5 %collective-permute-done.27.other_ref = bf16[2048,256]{1,0:T(8,128)(2,1)S(1)} collective-permute-done((bf16[2048,256]{1,0:T(8,128)(2,1)S(1)}, bf16[2048,256]{1,0:T(8,128)(2,1)S(1)}, u32[]{:S(2)}, u32[]{:S(2)}) %collective-permute-start.27) | collective-permute-done | bytes 1048608 | tf_op jit(solution)/shard_map/ppermute | solution.py:249
  174.6 9.6 %collective-permute-done.28 = bf16[2048,256]{1,0:T(8,128)(2,1)S(1)} collective-permute-done((bf16[2048,256]{1,0:T(8,128)(2,1)S(1)}, bf16[2048,256]{1,0:T(8,128)(2,1)S(1)}, u32[]{:S(2)}, u32[]{:S(2)}) %collective-permute-start.28) | collective-permute-done | bytes 1048608 | tf_op jit(solution)/shard_map/ppermute | solution.py:249
  189.2 26.1 %update_gram.1.gram_ref = f32[2048,4096]{1,0:T(8,128)} custom-call(s32[1]{0:T(128)} %bitcast.at_ref, f32[2048,4096]{1,0:T(8,128)} %gram_ref.5, bf16[256,6144]{1,0:T(8,128)(2,1)S(1)} %build_grads.1.left_ref.right_ref, bf16[256,6144]{1,0:T(8,128)(2,1)S(1)} %build_grads.1.left_ref.right_ref), custom_call_target="tpu_custom_call" | custom-call | flops 4294967296 | bytes 70254592 | tf_op jit(solution)/shard_map/update_gram/pallas_call | solution.py:133
  217.2 18.9 %moment.1 = f32[8,256]{1,0:T(8,128)S(1)} custom-call(s32[3]{0:T(128)S(1)} %pad_add_fusion.plan_ref, f32[2048,4096]{1,0:T(8,128)} %update_gram.1.gram_ref, bf16[2048,256]{1,0:T(8,128)(2,1)S(1)} %select_select_fusion.vec_ref, bf16[2048,256]{1,0:T(8,128)(2,1)S(1)} %copy-done.8, f32[2048,256]{1,0:T(8,128)S(1)} %copy-done.2), custom_call_target="tpu_custom_call" | custom-call | flops 4294967296 | bytes 37748736 | tf_op jit(solution)/shard_map/moment/pallas_call | solution.py:192
  237.4 3.6 %collective-permute-done.32 = f32[4,256]{1,0:T(4,128)S(1)} collective-permute-done((f32[4,256]{1,0:T(4,128)S(1)}, f32[4,256]{1,0:T(4,128)S(1)}, u32[]{:S(2)}, u32[]{:S(2)}) %collective-permute-start.32) | collective-permute-done | bytes 4128 | tf_op jit(solution)/shard_map/ppermute | solution.py:249
  242.6 2.1 collective-permute-done.33
  244.7 4.2 %collective-permute-start.34 = (f32[4,256]{1,0:T(4,128)S(1)}, f32[4,256]{1,0:T(4,128)S(1)}, u32[]{:S(2)}, u32[]{:S(2)}) collective-permute-start(f32[4,256]{1,0:T(4,128)S(1)} %add.143), channel_id=1, source_target_pairs={{0,8},{1,9},{2,10},{3,11},{4,12},{5,13},{6,14},{7,15},{8,0},{9,1},... | collective-permute-start | bytes 12296 | tf_op jit(solution)/shard_map/ppermute | solution.py:249
  250.6 5.0 %collective-permute-start.35 = (f32[4,256]{1,0:T(4,128)S(1)}, f32[4,256]{1,0:T(4,128)S(1)}, u32[]{:S(2)}, u32[]{:S(2)}) collective-permute-start(f32[4,256]{1,0:T(4,128)S(1)} %add.144), channel_id=1, source_target_pairs={{0,16},{1,17},{2,18},{3,19},{4,20},{5,21},{6,22},{7,23},{8,24},{9,... | collective-permute-start | bytes 12296 | tf_op jit(solution)/shard_map/ppermute | solution.py:249
  257.2 4.0 %multiply_subtract_fusion = f32[2048,256]{1,0:T(8,128)} fusion(f32[2048,256]{1,0:T(8,128)} %get-tuple-element.32.left_ref, f32[2048,256]{1,0:T(8,128)} %param.13, f32[256]{0:T(256)S(1)} %bitcast.91, f32[256]{0:T(256)S(1)} %bitcast.92), kind=kLoop, calls=%fused_computation.6 | loop fusion | flops 1572864 | bytes 6293504 | tf_op jit(solution)/shard_map/sub | solution.py:409
  (135 shorter events, 42.2 us)
Async XLA Ops:
  2.5 17.4 %collective-permute-start.15 = (bf16[2048,256]{1,0:T(8,128)(2,1)S(1)}, bf16[2048,256]{1,0:T(8,128)(2,1)}, u32[]{:S(2)}, u32[]{:S(2)}) collective-permute-start(bf16[2048,256]{1,0:T(8,128)(2,1)S(1)} %convert_element_type.31), channel_id=1, source_target_pairs={{0,8},{4,12},{9,17},{13,21},{18,26},{22,30}} | collective-permute-start | bytes 3145736 | tf_op jit(solution)/shard_map/ppermute | solution.py:249
  8.6 13.0 %collective-permute-start.12 = (bf16[2048,256]{1,0:T(8,128)(2,1)S(1)}, bf16[2048,256]{1,0:T(8,128)(2,1)}, u32[]{:S(2)}, u32[]{:S(2)}) collective-permute-start(bf16[2048,256]{1,0:T(8,128)(2,1)S(1)} %convert_element_type.31), channel_id=1, source_target_pairs={{9,1},{13,5},{18,10},{22,14},{27,19},{31,23}} | collective-permute-start | bytes 3145736 | tf_op jit(solution)/shard_map/ppermute | solution.py:249
  19.9 7.5 %collective-permute-start.16 = (bf16[2048,256]{1,0:T(8,128)(2,1)}, bf16[2048,256]{1,0:T(8,128)(2,1)}, u32[]{:S(2)}, u32[]{:S(2)}) collective-permute-start(bf16[2048,256]{1,0:T(8,128)(2,1)} %collective-permute-done.15), channel_id=1, source_target_pairs={{8,16},{12,20},{17,25},{21,29}} | collective-permute-start | bytes 3145736 | tf_op jit(solution)/shard_map/ppermute | solution.py:249
  21.6 7.4 %collective-permute-start.13 = (bf16[2048,256]{1,0:T(8,128)(2,1)}, bf16[2048,256]{1,0:T(8,128)(2,1)}, u32[]{:S(2)}, u32[]{:S(2)}) collective-permute-start(bf16[2048,256]{1,0:T(8,128)(2,1)} %collective-permute-done.12), channel_id=1, source_target_pairs={{10,2},{14,6},{19,11},{23,15}} | collective-permute-start | bytes 3145736 | tf_op jit(solution)/shard_map/ppermute | solution.py:249
  23.9 19.0 %collective-permute-start.6 = (bf16[256,128]{1,0:T(8,128)(2,1)S(1)}, bf16[256,128]{1,0:T(8,128)(2,1)S(1)}, u32[]{:S(2)}, u32[]{:S(2)}) collective-permute-start(bf16[256,128]{1,0:T(8,128)(2,1)S(1)} %convolution_convert_fusion), channel_id=1, source_target_pairs={{0,8},{1,9},{2,10},{3,11},{4,12},{5,13},{6,14},{7,15},{8,16},{9,17... | collective-permute-start | bytes 196616 | tf_op jit(solution)/shard_map/ppermute | solution.py:249
  27.4 50.0 %collective-permute-start.17 = (bf16[2048,256]{1,0:T(8,128)(2,1)}, bf16[2048,256]{1,0:T(8,128)(2,1)}, u32[]{:S(2)}, u32[]{:S(2)}) collective-permute-start(bf16[2048,256]{1,0:T(8,128)(2,1)} %collective-permute-done.16), channel_id=1, source_target_pairs={{16,24},{20,28}} | collective-permute-start | bytes 3145736 | tf_op jit(solution)/shard_map/ppermute | solution.py:249
  29.0 48.3 %collective-permute-start.14 = (bf16[2048,256]{1,0:T(8,128)(2,1)}, bf16[2048,256]{1,0:T(8,128)(2,1)}, u32[]{:S(2)}, u32[]{:S(2)}) collective-permute-start(bf16[2048,256]{1,0:T(8,128)(2,1)} %collective-permute-done.13), channel_id=1, source_target_pairs={{11,3},{15,7}} | collective-permute-start | bytes 3145736 | tf_op jit(solution)/shard_map/ppermute | solution.py:249
  33.1 12.9 %collective-permute-start = (bf16[2,128,128]{2,1,0:T(8,128)(2,1)S(1)}, bf16[2,128,128]{2,1,0:T(8,128)(2,1)S(1)}, u32[]{:S(2)}, u32[]{:S(2)}) collective-permute-start(bf16[2,128,128]{2,1,0:T(8,128)(2,1)S(1)} %bitcast.68), channel_id=1, source_target_pairs={{0,8},{1,9},{2,10},{3,11},{4,12},{5,13},{6,14},{7,15},{8,16},{9,17... | collective-permute-start | bytes 196616 | tf_op jit(solution)/shard_map/ppermute | solution.py:249
  42.9 6.4 %collective-permute-start.7 = (bf16[256,128]{1,0:T(8,128)(2,1)S(1)}, bf16[256,128]{1,0:T(8,128)(2,1)S(1)}, u32[]{:S(2)}, u32[]{:S(2)}) collective-permute-start(bf16[256,128]{1,0:T(8,128)(2,1)S(1)} %collective-permute-done.6), channel_id=1, source_target_pairs={{0,8},{1,9},{2,10},{3,11},{4,12},{5,13},{6,14},{7,15},{8,16},{9,17... | collective-permute-start | bytes 196616 | tf_op jit(solution)/shard_map/ppermute | solution.py:249
  46.0 15.2 %collective-permute-start.1 = (bf16[2,128,128]{2,1,0:T(8,128)(2,1)S(1)}, bf16[2,128,128]{2,1,0:T(8,128)(2,1)S(1)}, u32[]{:S(2)}, u32[]{:S(2)}) collective-permute-start(bf16[2,128,128]{2,1,0:T(8,128)(2,1)S(1)} %collective-permute-done), channel_id=1, source_target_pairs={{0,8},{1,9},{2,10},{3,11},{4,12},{5,13},{6,14},{7,15},{8,16},{9,17... | collective-permute-start | bytes 196616 | tf_op jit(solution)/shard_map/ppermute | solution.py:249
  49.3 12.6 %collective-permute-start.8 = (bf16[256,128]{1,0:T(8,128)(2,1)S(1)}, bf16[256,128]{1,0:T(8,128)(2,1)S(1)}, u32[]{:S(2)}, u32[]{:S(2)}) collective-permute-start(bf16[256,128]{1,0:T(8,128)(2,1)S(1)} %collective-permute-done.7), channel_id=1, source_target_pairs={{0,8},{1,9},{2,10},{3,11},{4,12},{5,13},{6,14},{7,15},{8,16},{9,17... | collective-permute-start | bytes 196616 | tf_op jit(solution)/shard_map/ppermute | solution.py:249
  61.2 6.1 %collective-permute-start.2 = (bf16[2,128,128]{2,1,0:T(8,128)(2,1)S(1)}, bf16[2,128,128]{2,1,0:T(8,128)(2,1)S(1)}, u32[]{:S(2)}, u32[]{:S(2)}) collective-permute-start(bf16[2,128,128]{2,1,0:T(8,128)(2,1)S(1)} %collective-permute-done.1), channel_id=1, source_target_pairs={{0,8},{1,9},{2,10},{3,11},{4,12},{5,13},{6,14},{7,15},{8,16},{9,17... | collective-permute-start | bytes 196616 | tf_op jit(solution)/shard_map/ppermute | solution.py:249
  61.9 7.9 %collective-permute-start.9 = (bf16[4,256,128]{2,1,0:T(8,128)(2,1)S(1)}, bf16[4,256,128]{2,1,0:T(8,128)(2,1)S(1)}, u32[]{:S(2)}, u32[]{:S(2)}) collective-permute-start(bf16[4,256,128]{2,1,0:T(8,128)(2,1)S(1)} %get-tuple-element.23), channel_id=1, source_target_pairs={{0,4},{1,5},{2,6},{3,7},{4,0},{5,1},{6,2},{7,3},{8,12},{9,13},{10,... | collective-permute-start | bytes 786440 | tf_op jit(solution)/shard_map/ppermute | solution.py:249
  67.3 6.5 %collective-permute-start.3 = (bf16[4,2,128,128]{3,2,1,0:T(8,128)(2,1)S(1)}, bf16[4,2,128,128]{3,2,1,0:T(8,128)(2,1)}, u32[]{:S(2)}, u32[]{:S(2)}) collective-permute-start(bf16[4,2,128,128]{3,2,1,0:T(8,128)(2,1)S(1)} %get-tuple-element.25), channel_id=1, source_target_pairs={{0,2},{1,3},{2,0},{3,1},{4,6},{5,7},{6,4},{7,5},{8,10},{9,11},{10,... | collective-permute-start | bytes 786440 | tf_op jit(solution)/shard_map/ppermute | solution.py:249
  70.9 21.5 %collective-permute-start.10 = (bf16[2,4,256,128]{3,2,1,0:T(8,128)(2,1)}, bf16[2,4,256,128]{3,2,1,0:T(8,128)(2,1)}, u32[]{:S(2)}, u32[]{:S(2)}) collective-permute-start(bf16[2,4,256,128]{3,2,1,0:T(8,128)(2,1)} %get-tuple-element.15), channel_id=1, source_target_pairs={{0,2},{1,3},{2,0},{3,1},{4,6},{5,7},{6,4},{7,5},{8,10},{9,11},{10,... | collective-permute-start | bytes 1572872 | tf_op jit(solution)/shard_map/ppermute | solution.py:249
  75.8 15.1 %collective-permute-start.4 = (bf16[2,4,2,128,128]{4,3,2,1,0:T(8,128)(2,1)}, bf16[2,4,2,128,128]{4,3,2,1,0:T(8,128)(2,1)}, u32[]{:S(2)}, u32[]{:S(2)}) collective-permute-start(bf16[2,4,2,128,128]{4,3,2,1,0:T(8,128)(2,1)} %get-tuple-element.17), channel_id=1, source_target_pairs={{0,4},{1,5},{2,6},{3,7},{4,0},{5,1},{6,2},{7,3},{8,12},{9,13},{10,... | collective-permute-start | bytes 1572872 | tf_op jit(solution)/shard_map/ppermute | solution.py:249
  77.8 26.8 %collective-permute-start.18 = (bf16[2048,256]{1,0:T(8,128)(2,1)S(1)}, bf16[2048,256]{1,0:T(8,128)(2,1)S(1)}, u32[]{:S(2)}, u32[]{:S(2)}) collective-permute-start(bf16[2048,256]{1,0:T(8,128)(2,1)S(1)} %select_select_fusion.1.vec_ref), channel_id=1, source_target_pairs={{0,4},{1,5},{2,6},{3,7},{4,0},{5,1},{6,2},{7,3},{8,12},{9,13},{10,... | collective-permute-start | bytes 3145736 | tf_op jit(solution)/shard_map/ppermute | solution.py:249
  92.3 23.4 %collective-permute-start.5 = (bf16[2,2,4,2,128,128]{5,4,3,2,1,0:T(8,128)(2,1)S(1)}, bf16[2,2,4,2,128,128]{5,4,3,2,1,0:T(8,128)(2,1)S(1)}, u32[]{:S(2)}, u32[]{:S(2)}) collective-permute-start(bf16[2,2,4,2,128,128]{5,4,3,2,1,0:T(8,128)(2,1)S(1)} %get-tuple-element.13), channel_id=1, source_target_pairs={{0,1},{1,0},{2,3},{3,2},{4,5},{5,4},{6,7},{7,6},{8,9},{9,8},{10,11... | collective-permute-start | bytes 3145736 | tf_op jit(solution)/shard_map/ppermute | solution.py:249
  93.6 22.6 %collective-permute-start.11 = (bf16[2,2,4,256,128]{4,3,2,1,0:T(8,128)(2,1)S(1)}, bf16[2,2,4,256,128]{4,3,2,1,0:T(8,128)(2,1)S(1)}, u32[]{:S(2)}, u32[]{:S(2)}) collective-permute-start(bf16[2,2,4,256,128]{4,3,2,1,0:T(8,128)(2,1)S(1)} %get-tuple-element.11), channel_id=1, source_target_pairs={{0,1},{1,0},{2,3},{3,2},{4,5},{5,4},{6,7},{7,6},{8,9},{9,8},{10,11... | collective-permute-start | bytes 3145736 | tf_op jit(solution)/shard_map/ppermute | solution.py:249
  115.6 5.9 %collective-permute-start.19 = (f32[1024,256]{1,0:T(8,128)S(1)}, f32[1024,256]{1,0:T(8,128)S(1)}, u32[]{:S(2)}, u32[]{:S(2)}) collective-permute-start(f32[1024,256]{1,0:T(8,128)S(1)} %constant_dynamic-slice_fusion.4), channel_id=1, source_target_pairs={{0,1},{1,0},{2,3},{3,2},{4,5},{5,4},{6,7},{7,6},{8,9},{9,8},{10,11... | collective-permute-start | bytes 3145736 | tf_op jit(solution)/shard_map/ppermute | solution.py:249
  121.6 14.4 %collective-permute-start.20 = (bf16[1024,256]{1,0:T(8,128)(2,1)S(1)}, bf16[1024,256]{1,0:T(8,128)(2,1)S(1)}, u32[]{:S(2)}, u32[]{:S(2)}) collective-permute-start(bf16[1024,256]{1,0:T(8,128)(2,1)S(1)} %add_convert_fusion), channel_id=1, source_target_pairs={{0,2},{1,3},{2,0},{3,1},{4,6},{5,7},{6,4},{7,5},{8,10},{9,11},{10,... | collective-permute-start | bytes 1572872 | tf_op jit(solution)/shard_map/ppermute | solution.py:249
  122.2 14.8 %collective-permute-start.22 = (f32[2,2,64,256]{3,2,1,0:T(8,128)S(1)}, f32[2,2,64,256]{3,2,1,0:T(8,128)S(1)}, u32[]{:S(2)}, u32[]{:S(2)}) collective-permute-start(f32[2,2,64,256]{3,2,1,0:T(8,128)S(1)} %pad_maximum_fusion.8), channel_id=1, source_target_pairs={{0,1},{1,0},{2,3},{3,2},{4,5},{5,4},{6,7},{7,6},{8,9},{9,8},{10,11... | collective-permute-start | bytes 786440 | tf_op jit(solution)/shard_map/ppermute | solution.py:249
  137.0 11.6 %collective-permute-start.21 = (f32[1024,256]{1,0:T(8,128)}, f32[1024,256]{1,0:T(8,128)}, u32[]{:S(2)}, u32[]{:S(2)}) collective-permute-start(f32[1024,256]{1,0:T(8,128)} %convert_add_fusion), channel_id=1, source_target_pairs={{0,1},{1,0},{2,3},{3,2},{4,5},{5,4},{6,7},{7,6},{8,9},{9,8},{10,11... | collective-permute-start | bytes 3145736 | tf_op jit(solution)/shard_map/ppermute | solution.py:249
  138.5 9.0 %collective-permute-start.23 = (f32[2,2,64,256]{3,2,1,0:T(8,128)}, f32[2,2,64,256]{3,2,1,0:T(8,128)}, u32[]{:S(2)}, u32[]{:S(2)}) collective-permute-start(f32[2,2,64,256]{3,2,1,0:T(8,128)} %fusion.27), channel_id=1, source_target_pairs={{0,2},{1,3},{2,0},{3,1},{4,6},{5,7},{6,4},{7,5},{8,10},{9,11},{10,... | collective-permute-start | bytes 786440 | tf_op jit(solution)/shard_map/ppermute | solution.py:249
  153.9 16.7 %collective-permute-start.27 = (bf16[2048,256]{1,0:T(8,128)(2,1)S(1)}, bf16[2048,256]{1,0:T(8,128)(2,1)S(1)}, u32[]{:S(2)}, u32[]{:S(2)}) collective-permute-start(bf16[2048,256]{1,0:T(8,128)(2,1)S(1)} %get-tuple-element.9), channel_id=1, source_target_pairs={{0,4},{4,0},{9,13},{13,9},{18,22},{22,18},{27,31},{31,27}} | collective-permute-start | bytes 3145736 | tf_op jit(solution)/shard_map/ppermute | solution.py:249
  157.3 15.6 %collective-permute-start.24 = (bf16[2048,256]{1,0:T(8,128)(2,1)S(1)}, bf16[2048,256]{1,0:T(8,128)(2,1)S(1)}, u32[]{:S(2)}, u32[]{:S(2)}) collective-permute-start(bf16[2048,256]{1,0:T(8,128)(2,1)S(1)} %get-tuple-element.9), channel_id=1, source_target_pairs={{9,1},{13,5},{18,10},{22,14},{27,19},{31,23}} | collective-permute-start | bytes 3145736 | tf_op jit(solution)/shard_map/ppermute | solution.py:249
  170.6 13.6 %collective-permute-start.28 = (bf16[2048,256]{1,0:T(8,128)(2,1)S(1)}, bf16[2048,256]{1,0:T(8,128)(2,1)S(1)}, u32[]{:S(2)}, u32[]{:S(2)}) collective-permute-start(bf16[2048,256]{1,0:T(8,128)(2,1)S(1)} %collective-permute-done.27.other_ref), channel_id=1, source_target_pairs={{0,8},{4,12},{9,17},{13,21},{18,26},{22,30}} | collective-permute-start | bytes 3145736 | tf_op jit(solution)/shard_map/ppermute | solution.py:249
  172.9 12.9 %collective-permute-start.25 = (bf16[2048,256]{1,0:T(8,128)(2,1)S(1)}, bf16[2048,256]{1,0:T(8,128)(2,1)}, u32[]{:S(2)}, u32[]{:S(2)}) collective-permute-start(bf16[2048,256]{1,0:T(8,128)(2,1)S(1)} %collective-permute-done.24), channel_id=1, source_target_pairs={{10,2},{14,6},{19,11},{23,15}} | collective-permute-start | bytes 3145736 | tf_op jit(solution)/shard_map/ppermute | solution.py:249
  185.8 29.5 %collective-permute-start.26 = (bf16[2048,256]{1,0:T(8,128)(2,1)}, bf16[2048,256]{1,0:T(8,128)(2,1)}, u32[]{:S(2)}, u32[]{:S(2)}) collective-permute-start(bf16[2048,256]{1,0:T(8,128)(2,1)} %collective-permute-done.25), channel_id=1, source_target_pairs={{11,3},{15,7}} | collective-permute-start | bytes 3145736 | tf_op jit(solution)/shard_map/ppermute | solution.py:249
  187.4 27.9 %collective-permute-start.30 = (bf16[2048,256]{1,0:T(8,128)(2,1)}, bf16[2048,256]{1,0:T(8,128)(2,1)}, u32[]{:S(2)}, u32[]{:S(2)}) collective-permute-start(bf16[2048,256]{1,0:T(8,128)(2,1)} %collective-permute-done.29), channel_id=1, source_target_pairs={{16,24},{20,28}} | collective-permute-start | bytes 3145736 | tf_op jit(solution)/shard_map/ppermute | solution.py:249
  244.7 5.8 %collective-permute-start.34 = (f32[4,256]{1,0:T(4,128)S(1)}, f32[4,256]{1,0:T(4,128)S(1)}, u32[]{:S(2)}, u32[]{:S(2)}) collective-permute-start(f32[4,256]{1,0:T(4,128)S(1)} %add.143), channel_id=1, source_target_pairs={{0,8},{1,9},{2,10},{3,11},{4,12},{5,13},{6,14},{7,15},{8,0},{9,1},... | collective-permute-start | bytes 12296 | tf_op jit(solution)/shard_map/ppermute | solution.py:249
  250.6 6.6 %collective-permute-start.35 = (f32[4,256]{1,0:T(4,128)S(1)}, f32[4,256]{1,0:T(4,128)S(1)}, u32[]{:S(2)}, u32[]{:S(2)}) collective-permute-start(f32[4,256]{1,0:T(4,128)S(1)} %add.144), channel_id=1, source_target_pairs={{0,16},{1,17},{2,18},{3,19},{4,20},{5,21},{6,22},{7,23},{8,24},{9,... | collective-permute-start | bytes 12296 | tf_op jit(solution)/shard_map/ppermute | solution.py:249
  (25 other events, 308.9 us)
